TPU v7x, 32 devices: a whole 2x2x4 slice. The times are simulated.
32 devices in a mesh: img: 8 (over z, x), pose: 4 (over y, core).
Axes of the slice: x: 2, y: 2, z: 4, core: 2. Of those that a mesh axis runs over, the one named last changes fastest.
Arguments:
- images: bfloat16 [2048, 4096], P('img'), may hold values from -100 to 100
- inv_noise: float32 [2048], P('img'), may hold values from 0.5 to 2
- defocus_class: int32 [2048], P('img'), may hold values from 0 to 15
- defocus: float32 [16], replicated, may hold values from 1 to 3
- pose_dir: int32 [512], P('pose'), may hold values from 0 to 503
- pose_shift: int32 [512, 2], P('pose'), may hold values from -8 to 8
- slabs: float32 [64, 4096], P('img', 'pose'), may hold values from -0.5 to 0.5
Outputs:
- slabs_out: float32 [64, 4096], P('img', 'pose')
- evidence: float32 [2048], P(('img', 'pose'))
All inputs are finite; a program needn't handle non-finite values.
Results may differ from a plain program's by a relative error of at most 0.0027.
Values sent between devices are 32-bit elements; how exact they have to be, the bound alone decides.
A program may use at most 64 MiB of HBM per device.

v0:
```python
import math

import jax
import jax.numpy as jnp
from jax import lax
from jax.sharding import PartitionSpec as P

NS = 64
KW = 64
KH = 32
CLASSES = 16
STEPS = 2


highest_precision = lax.Precision.HIGHEST


def coefficient_freqs():
    position = jnp.arange(KW * KH, dtype=jnp.int32)
    freq_x = (position % KW - KW // 2).astype(jnp.float32)
    freq_y = (position // KW).astype(jnp.float32)
    return (freq_x, freq_y)


def ctf_values(defocus):
    freq_x, freq_y = coefficient_freqs()
    radius_sq = (freq_x * freq_x + freq_y * freq_y) / (KH * KH)
    transfer = -jnp.sin(8.0 * defocus[:, None] * radius_sq[None, :] + 0.1)
    return jnp.concatenate([transfer, transfer], axis=1)


def slab_weights(pose_dir):
    lower = pose_dir // 8
    fraction = (pose_dir % 8).astype(jnp.float32) / 8.0
    slab_ids = jnp.arange(NS, dtype=jnp.int32)
    first = jnp.where(
        slab_ids[None, :] == lower[:, None], 1.0 - fraction[:, None], 0.0 * fraction[:, None]
    )
    second = jnp.where(
        slab_ids[None, :] == lower[:, None] + 1, fraction[:, None], 0.0 * fraction[:, None]
    )
    return first + second


def rotate(values, pose_shift, direction):
    freq_x, freq_y = coefficient_freqs()
    shift_x = pose_shift[:, 0:1].astype(jnp.float32)
    shift_y = pose_shift[:, 1:2].astype(jnp.float32)
    angles = 2.0 * math.pi / (4 * KH) * (shift_x * freq_x[None, :] + shift_y * freq_y[None, :])
    cosine = jnp.cos(angles)
    sine = direction * jnp.sin(angles)
    half_width = KW * KH
    real_part = values[:, :half_width]
    imag_part = values[:, half_width:]
    return jnp.concatenate(
        [real_part * cosine - imag_part * sine, real_part * sine + imag_part * cosine], axis=1
    )


def weight_images(images, class_onehot, table):
    image_ctf = jnp.dot(
        class_onehot, table, precision=highest_precision, preferred_element_type=jnp.float32
    )
    return image_ctf * images.astype(jnp.float32)


def tile_scores(references, weighted, ctf_sq, class_onehot, inv_noise):
    ref_sq = references * references
    energy = lax.dot_general(
        ctf_sq,
        ref_sq,
        (((1,), (1,)), ((), ())),
        precision=highest_precision,
        preferred_element_type=jnp.float32,
    )
    picked = jnp.dot(
        class_onehot, energy, precision=highest_precision, preferred_element_type=jnp.float32
    )
    inner = lax.dot_general(
        weighted,
        references,
        (((1,), (1,)), ((), ())),
        precision=highest_precision,
        preferred_element_type=jnp.float32,
    )
    return inv_noise[:, None] * (inner - 0.5 * picked)


def pose_evidence(scores):
    peak = lax.pmax(jnp.max(scores, axis=1), "pose")
    total = lax.psum(jnp.sum(jnp.exp(scores - peak[:, None]), axis=1), "pose")
    return peak + jnp.log(total)


def pose_pull(scores, log_total, inv_noise, weighted, class_onehot):
    usage = (inv_noise[:, None] * jnp.exp(scores - log_total[:, None])).astype(jnp.bfloat16)
    pull = lax.dot_general(
        usage.astype(jnp.float32),
        weighted,
        (((0,), (0,)), ((), ())),
        precision=highest_precision,
        preferred_element_type=jnp.float32,
    )
    mass = lax.dot_general(
        usage,
        class_onehot.astype(jnp.bfloat16),
        (((0,), (0,)), ((), ())),
        preferred_element_type=jnp.float32,
    )
    return (pull, mass)


def slab_gradient(weights_mat, plain, pull, mass, pose_shift, ctf_sq):
    damping = jnp.dot(mass, ctf_sq, precision=highest_precision, preferred_element_type=jnp.float32)
    backward = rotate(pull, pose_shift, -1.0) - plain * damping
    return lax.dot_general(
        weights_mat,
        backward,
        (((0,), (0,)), ((), ())),
        precision=highest_precision,
        preferred_element_type=jnp.float32,
    )


def assemble(own_map):
    columns = lax.all_gather(own_map, "pose", axis=1, tiled=True)
    return lax.all_gather(columns, "img", axis=0, tiled=True)


def shards(images, inv_noise, defocus_class, defocus, pose_dir, pose_shift, slabs):
    table = ctf_values(defocus)
    ctf_sq = table * table
    class_onehot = (defocus_class[:, None] == jnp.arange(CLASSES, dtype=jnp.int32)[None, :]).astype(
        jnp.float32
    )
    weighted = weight_images(images, class_onehot, table)
    weights_mat = slab_weights(pose_dir)
    slab_map = assemble(slabs)
    for step_index in range(STEPS):
        plain = jnp.dot(
            weights_mat, slab_map, precision=highest_precision, preferred_element_type=jnp.float32
        )
        references = rotate(plain, pose_shift, 1.0)
        scores = tile_scores(references, weighted, ctf_sq, class_onehot, inv_noise)
        log_total = pose_evidence(scores)
        pull, mass = pose_pull(scores, log_total, inv_noise, weighted, class_onehot)
        gradient = slab_gradient(weights_mat, plain, pull, mass, pose_shift, ctf_sq)
        evidence = log_total
        whole = lax.psum(gradient, ("img", "pose"))
        spread = jnp.sqrt(jnp.mean(whole * whole) + 1e-06)
        slab_map = slab_map + 0.05 * whole / spread
    row_count = slab_map.shape[0] // lax.axis_size("img")
    column_count = slab_map.shape[1] // lax.axis_size("pose")
    own_map = lax.dynamic_slice(
        slab_map,
        (lax.axis_index("img") * row_count, lax.axis_index("pose") * column_count),
        (row_count, column_count),
    )
    share = evidence.shape[0] // lax.axis_size("pose")
    own_evidence = lax.dynamic_slice_in_dim(evidence, lax.axis_index("pose") * share, share, 0)
    return (own_map, own_evidence)


def solution(mesh):
    in_specs = (
        P("img", None),
        P("img"),
        P("img"),
        P(),
        P("pose"),
        P("pose", None),
        P("img", "pose"),
    )
    out_specs = (P("img", "pose"), P(("img", "pose")))
    return jax.shard_map(shards, mesh=mesh, in_specs=in_specs, out_specs=out_specs, check_vma=False)
```

profile of v0, /device:TPU:0, one launch (start us, length us, event | category | flops | bytes accessed | tf_op | source)
XLA Modules:
  0.0 404.9 jit_solution(9004261728012027666)
XLA Ops:
  7.2 8.4 %all_gather.6 = f32[8,4096]{1,0:T(8,128)} all-gather(f32[8,1024]{1,0:T(8,128)} %param.13), channel_id=1, replica_groups=mesh['img'=8,'pose'=4] {'pose'}, dimensions={1}, use_global_device_ids=true | all-gather | bytes 163840 | tf_op jit(solution)/shard_map/all_gather | solution.py:126
  16.3 0.7 broadcast_subtract_fusion
  17.0 0.7 broadcast_add_fusion
  17.7 0.8 convert_bitcast_fusion.1
  18.9 5.5 %convolution_multiply_fusion = f32[256,4096]{1,0:T(8,128)} fusion(bf16[256,4096]{1,0:T(8,128)(2,1)} %param.7, f32[16,2048]{1,0:T(8,128)S(1)} %sine_negate_fusion, s32[256]{0:T(256)} %param.9), kind=kOutput, calls=%fused_computation | convolution fusion | flops 203493376 | bytes 6423552 | tf_op jit(solution)/shard_map/dot_general | solution.py:61
  24.4 31.9 %all-gather.2.cloned.1.call-done = f32[64,4096]{1,0:T(8,128)} async-done(((f32[8,4096]{1,0:T(8,128)}), f32[64,4096]{1,0:T(8,128)}) %all-gather.2.cloned.1.call-update) | async-done | bytes 1048592 | tf_op jit(solution)/shard_map/all_gather | solution.py:127
  56.3 3.1 fusion.30
  59.5 4.1 %multiply_subtract_fusion.3 = (f32[128,2048]{1,0:T(8,128)S(1)}, f32[128,2048]{1,0:T(8,128)S(1)}) fusion(f32[128,4096]{1,0:T(8,128)S(1)} %fusion.30, f32[2048]{0:T(1024)S(1)} %get-tuple-element.22, f32[128]{0:T(128)S(1)} %get-tuple-element.15, f32[2048]{0:T(1024)S(1)} %get-tuple-element.23, f32[128]{0:T(128)S(1)} %get-tuple-element.14), kind=kLoop, calls=%fused_computation.29 | loop fusion | flops 2621440 | bytes 4211712 | tf_op jit(solution)/shard_map/sub | solution.py:56
  63.6 1.7 fusion.4
  65.4 4.3 %fusion.7 = f32[256,128]{0,1:T(8,128)S(1)} fusion(f32[256,4096]{1,0:T(8,128)S(1)} %copy-done, f32[128,2048]{1,0:T(8,128)S(1)} %get-tuple-element.13, f32[128,2048]{1,0:T(8,128)S(1)} %get-tuple-element.12), kind=kOutput, calls=%fused_computation.12 | convolution fusion | flops 1611137024 | bytes 6422528 | tf_op jit(solution)/shard_map/dot_general | solution.py:79
  70.0 5.7 %pmax.14 = f32[256]{0:T(256)S(1)} all-reduce(f32[256]{0:T(256)S(1)} %get-tuple-element.18), channel_id=1, replica_groups=mesh['img'=8,'pose'=4] {'pose'}, use_global_device_ids=true, to_apply=%region_1.2 | all-reduce | flops 256 | bytes 2048 | tf_op jit(solution)/shard_map/pmax | solution.py:90
  75.7 6.8 %psum.28 = f32[256]{0:T(256)S(1)} all-reduce(f32[256]{0:T(256)S(1)} %exponential_reduce_fusion.1), channel_id=1, replica_groups=mesh['img'=8,'pose'=4] {'pose'}, use_global_device_ids=true, to_apply=%region_3.4 | all-reduce | flops 256 | bytes 2048 | tf_op jit(solution)/shard_map/psum | solution.py:91
  82.7 3.9 fusion.56
  86.6 4.2 %multiply_subtract_fusion.2 = (f32[128,2048]{1,0:T(8,128)S(1)}, f32[128,2048]{1,0:T(8,128)S(1)}) fusion(f32[128,4096]{1,0:T(8,128)S(1)} %fusion.56, f32[2048]{0:T(1024)S(1)} %get-tuple-element.22, f32[128]{0:T(128)S(1)} %get-tuple-element.15, f32[2048]{0:T(1024)S(1)} %get-tuple-element.23, f32[128]{0:T(128)S(1)} %get-tuple-element.14), kind=kLoop, calls=%fused_computation.27 | loop fusion | flops 2883584 | bytes 4211712 | tf_op jit(solution)/shard_map/sub | solution.py:56
  90.8 2.0 fusion.1
  92.8 2.3 fusion.29
  95.4 127.9 %all-reduce.3.cloned.1.call-done = f32[64,4096]{1,0:T(8,128)} async-done(((f32[64,4096]{1,0:T(8,128)}), f32[64,4096]{1,0:T(8,128)}) %all-reduce.3.cloned.1.call-update) | async-done | bytes 1048592 | tf_op jit(solution)/shard_map/psum | solution.py:149
  223.3 2.1 multiply_reduce_fusion.1
  226.1 1.3 divide_add_fusion
  227.4 1.9 fusion.28
  229.3 4.1 %multiply_subtract_fusion.1 = (f32[128,2048]{1,0:T(8,128)S(1)}, f32[128,2048]{1,0:T(8,128)S(1)}) fusion(f32[128,4096]{1,0:T(8,128)S(1)} %fusion.28, f32[2048]{0:T(1024)S(1)} %get-tuple-element.22, f32[128]{0:T(128)S(1)} %get-tuple-element.15, f32[2048]{0:T(1024)S(1)} %get-tuple-element.23, f32[128]{0:T(128)S(1)} %get-tuple-element.14), kind=kLoop, calls=%fused_computation.23 | loop fusion | flops 2621440 | bytes 4211712 | tf_op jit(solution)/shard_map/sub | solution.py:56
  233.5 4.3 %fusion.6 = f32[256,128]{0,1:T(8,128)S(1)} fusion(f32[256,4096]{1,0:T(8,128)S(1)} %copy-done.1, f32[128,2048]{1,0:T(8,128)S(1)} %get-tuple-element.9, f32[128,2048]{1,0:T(8,128)S(1)} %get-tuple-element.8), kind=kOutput, calls=%fused_computation.11 | convolution fusion | flops 1611137024 | bytes 6422528 | tf_op jit(solution)/shard_map/dot_general | solution.py:79
  237.7 1.7 fusion.2
  239.8 5.7 %pmax.15 = f32[256]{0:T(256)S(1)} all-reduce(f32[256]{0:T(256)S(1)} %get-tuple-element.20), channel_id=1, replica_groups=mesh['img'=8,'pose'=4] {'pose'}, use_global_device_ids=true, to_apply=%region_7.8 | all-reduce | flops 256 | bytes 2048 | tf_op jit(solution)/shard_map/pmax | solution.py:90
  245.5 6.8 %psum.30 = f32[256]{0:T(256)S(1)} all-reduce(f32[256]{0:T(256)S(1)} %exponential_reduce_fusion), channel_id=1, replica_groups=mesh['img'=8,'pose'=4] {'pose'}, use_global_device_ids=true, to_apply=%region_9.10 | all-reduce | flops 256 | bytes 2048 | tf_op jit(solution)/shard_map/psum | solution.py:91
  252.6 3.9 fusion.57
  256.5 4.2 %multiply_subtract_fusion = (f32[128,2048]{1,0:T(8,128)S(1)}, f32[128,2048]{1,0:T(8,128)S(1)}) fusion(f32[128,4096]{1,0:T(8,128)S(1)} %fusion.57, f32[2048]{0:T(1024)S(1)} %get-tuple-element.22, f32[128]{0:T(128)S(1)} %get-tuple-element.15, f32[2048]{0:T(1024)S(1)} %get-tuple-element.23, f32[128]{0:T(128)S(1)} %get-tuple-element.14), kind=kLoop, calls=%fused_computation.21 | loop fusion | flops 2883584 | bytes 4211712 | tf_op jit(solution)/shard_map/sub | solution.py:56
  260.7 2.0 fusion
  262.7 2.4 fusion.27
  265.7 128.6 %all-reduce.5.cloned.1.call-done = f32[64,4096]{1,0:T(8,128)} async-done(((f32[64,4096]{1,0:T(8,128)}), f32[64,4096]{1,0:T(8,128)}) %all-reduce.5.cloned.1.call-update) | async-done | bytes 1048592 | tf_op jit(solution)/shard_map/psum | solution.py:149
  394.2 2.1 multiply_reduce_fusion
  397.0 1.4 dynamic-slice_add_fusion
  (30 shorter events, 3.5 us)
Async XLA Ops:
  7.2 49.2 %all-gather.2.cloned.1.call-start = ((), (), s32[]{:S(2)}) async-start(), calls=%async_computation | async-start | bytes 1179648 | tf_op jit(solution)/shard_map/all_gather | solution.py:127
  15.6 207.7 %all-reduce.3.cloned.1.call-start = ((), (), s32[]{:S(2)}) async-start(), calls=%async_computation.1 | async-start | bytes 2097152 | tf_op jit(solution)/shard_map/psum | solution.py:149
  59.4 5.9 %copy-start = (f32[256,4096]{1,0:T(8,128)S(1)}, f32[256,4096]{1,0:T(8,128)}, u32[]{:S(2)}) copy-start(f32[256,4096]{1,0:T(8,128)} %convolution_multiply_fusion) | copy-start | bytes 12582916
  65.3 4.3 %copy-start.3 = (f32[256]{0:T(256)S(1)}, f32[256]{0:T(256)}, u32[]{:S(2)}) copy-start(f32[256]{0:T(256)} %param.8) | copy-start | bytes 3076
  65.4 4.3 %copy-start.4 = (s32[256]{0:T(256)S(1)}, s32[256]{0:T(256)}, u32[]{:S(2)}) copy-start(s32[256]{0:T(256)} %param.9) | copy-start | bytes 3076
  92.8 133.3 %copy-start.2 = (f32[64,4096]{1,0:T(8,128)S(1)}, f32[64,4096]{1,0:T(8,128)}, u32[]{:S(2)}) copy-start(f32[64,4096]{1,0:T(8,128)} %all-gather.2.cloned.1.call-done) | copy-start | bytes 3145732
  95.1 299.1 %all-reduce.5.cloned.1.call-start = ((), (), s32[]{:S(2)}) async-start(), calls=%async_computation.2 | async-start | bytes 2097152 | tf_op jit(solution)/shard_map/psum | solution.py:149
  229.3 4.2 %copy-start.1 = (f32[256,4096]{1,0:T(8,128)S(1)}, f32[256,4096]{1,0:T(8,128)}, u32[]{:S(2)}) copy-start(f32[256,4096]{1,0:T(8,128)} %convolution_multiply_fusion) | copy-start | bytes 12582916
Sparse Core Ops, SparseCore 0:
  15.7 40.5 all-gather.1
  95.3 127.9 all-reduce.2
  265.2 129.0 all-reduce.4
where the time goes:
time: 406 us; the launch traced here: 405 us
  waiting for transfers between devices  288 us (71%)
  matrix products  40 us (10%)
  blocking collectives  33.3 us (8%)
  other arithmetic  26.9 us (7%)
  between operations  15.3 us (4%)
    psum x2, waiting for transfers between devices, shards(): whole = lax.psum(gradient, ('img', 'pose'))  256 us
    all_gather x1, waiting for transfers between devices, assemble(): return lax.all_gather(columns, 'img', axis=0, tiled=True)  31.9 us
    sub x4, other arithmetic, rotate(): real_part * cosine - imag_part * sine  16.6 us
    psum x2, blocking collectives, pose_evidence(): total = lax.psum(jnp.sum(jnp.exp(scores - peak[:, None]), axis=1), 'pose')  13.6 us
    pmax x2, blocking collectives, pose_evidence(): peak = lax.pmax(jnp.max(scores, axis=1), 'pose')  11.3 us
    dot_general x2, matrix products, tile_scores(): lax.dot_general(weighted, references, (((1,), (1,)), ((), ())), precision...  8.52 us
    all_gather x1, blocking collectives, assemble(): columns = lax.all_gather(own_map, 'pose', axis=1, tiled=True)  8.37 us
  transfers between devices with their start and end apart: 3, of which 3 were waited for; matrix products, arithmetic and copies ran while one was open for 2% of the time, Pallas kernels for 0%

commit v1 on v0

v1 whole, which is shorter than its diff:
```python
import functools
import math

import jax
import jax.numpy as jnp
from jax import lax
from jax.experimental import pallas as pl
from jax.experimental.pallas import tpu as pltpu
from jax.sharding import PartitionSpec as P

NS = 64
KW = 64
KH = 32
F = KW * KH * 2
CLASSES = 16
STEPS = 2
BW = 256
NB = F // BW
HB = NB // 2
F32 = jnp.float32
BF = jnp.bfloat16
MESH = pl.DeviceIdType.MESH


def dot(a, b):
    return jnp.dot(a, b, preferred_element_type=F32)


def dot_t(a, b):
    return lax.dot_general(a, b, (((1,), (1,)), ((), ())), preferred_element_type=F32)


def split2(v):
    hi = v.astype(BF)
    lo = (v - hi.astype(F32)).astype(BF)
    return hi, lo


def split3(v):
    hi = v.astype(BF)
    rest = v - hi.astype(F32)
    mid = rest.astype(BF)
    lo = (rest - mid.astype(F32)).astype(BF)
    return hi, mid, lo


def kernel(
    dims,
    img_ref, noise_ref, class_ref, defocus_ref, dir_ref, shift_ref, slab_ref,
    out_ref, ev_ref,
    wh, wl, cosr, sinr, csq, plain, m0, m1, grad, ra, s1, rb, s2, rc, own,
    ebuf, ta, tb, tc, sc_acc, en_acc, use_ref, mass_ref,
    ag_s, ag_r, rs_s, rs_r, ev_s, ev_r, t_s, t_r,
):
    (X, Z, U, R, K, KC) = dims
    KB = K // KC
    NI = img_ref.shape[0]
    NP = dir_ref.shape[1]
    NPOSE = 2 * U
    i = lax.axis_index("img")
    p = lax.axis_index("pose")
    z, x = lax.div(i, X), lax.rem(i, X)
    u, c = lax.div(p, 2), lax.rem(p, 2)

    def coords(off):
        dz, dx, du, dc = off
        return (lax.rem(z + dz, Z), lax.rem(x + dx, X), lax.rem(u + du, U), lax.rem(c + dc, 2))

    def device(co):
        return (co[0] * X + co[1], co[2] * 2 + co[3])

    offs_a = [(0, 0, 0, 1)]
    offs_b = [(0, dx, du, 0) for du in range(U) for dx in range(X) if du or dx]
    offs_c = [(dz, 0, 0, 0) for dz in range(1, Z)]
    offs_e = [(0, 0, du, dc) for du in range(U) for dc in range(2) if du or dc]
    everyone = sorted(set(offs_a + offs_b + offs_c + offs_e))
    nb, nc = len(offs_b), len(offs_c)

    barrier = pltpu.get_barrier_semaphore()
    for off in everyone:
        pl.semaphore_signal(barrier, inc=1, device_id=device(coords(off)), device_id_type=MESH)
    pl.semaphore_wait(barrier, len(everyone))

    def send(src, dst, ss, rs, off):
        d = pltpu.make_async_remote_copy(
            src_ref=src, dst_ref=dst, send_sem=ss, recv_sem=rs,
            device_id=device(coords(off)), device_id_type=MESH,
        )
        d.start()
        return d

    pend = []

    def gather_start(m, g):
        return [
            send(m.at[c, :, u, x, z], m.at[c, :, u, x, z], ag_s.at[g, n], ag_r.at[g, n], off)
            for n, off in enumerate(offs_c)
        ]

    def gather_b(m, g, first):
        for d in first:
            d.wait_recv()
        pend.extend(first)
        return [
            send(m.at[c, :, u, x], m.at[c, :, u, x], ag_s.at[g, nc + n], ag_r.at[g, nc + n], off)
            for n, off in enumerate(offs_b)
        ]

    def gather_a(m, g, second):
        for d in second:
            d.wait_recv()
        pend.extend(second)
        return send(m.at[c], m.at[c], ag_s.at[g, nc + nb], ag_r.at[g, nc + nb], offs_a[0])

    for k in range(K):
        m0[c, k, u, x, z] = slab_ref[:, k * BW:(k + 1) * BW]
    first = gather_start(m0, 0)

    row_r = lax.broadcasted_iota(jnp.int32, (128, NI), 0)
    class_row = class_ref[...]
    hot = jnp.where(row_r % CLASSES == class_row, 1.0, 0.0)
    hot3 = jnp.where(row_r < 3 * CLASSES, hot, 0.0)
    pick = jnp.where((row_r < CLASSES) | ((row_r >= 2 * CLASSES) & (row_r < 3 * CLASSES)), hot, 0.0).astype(BF)
    hot3_t = hot3.T.astype(BF)

    srow = lax.broadcasted_iota(jnp.int32, (128, NP), 0)
    sx_ = lax.div(srow, Z * R)
    sz_ = lax.rem(lax.div(srow, R), Z)
    slab_id = jnp.where(srow < NS, (sz_ * X + sx_) * R + lax.rem(srow, R), -5)
    pdir = dir_ref[...]
    lower = lax.div(pdir, 8)
    frac = lax.rem(pdir, 8).astype(F32) / 8.0
    wt = jnp.where(slab_id == lower, 1.0 - frac, 0.0) + jnp.where(slab_id == lower + 1, frac, 0.0)
    w_t = wt[:NS].astype(BF)
    w_t2 = jnp.concatenate([w_t, w_t], axis=1)
    w = wt.T[:, :NS]
    w3 = jnp.concatenate([w, w, w], axis=1).astype(BF)

    first = gather_b(m0, 0, first)

    lane = lax.broadcasted_iota(jnp.int32, (NP, 128), 1)
    shx = shift_ref[:, 0:1]
    shy = shift_ref[:, 1:2]
    turn = 2.0 * math.pi / (4 * KH)
    base = turn * (shx * (lane % KW - KW // 2) + shy * lax.div(lane, KW)).astype(F32)
    inc = turn * (2 * shy + 0 * lane).astype(F32)
    cb, sb, ci, si = jnp.cos(base), jnp.sin(base), jnp.cos(inc), jnp.sin(inc)
    for t in range(KW * KH // 128):
        b, h = (t * 128) // BW, (t * 128) % BW
        cosr[b, :, h:h + 128] = cb
        sinr[b, :, h:h + 128] = sb
        cb, sb = cb * ci - sb * si, sb * ci + cb * si

    for b in range(HB):
        pos = lax.broadcasted_iota(jnp.int32, (CLASSES, BW), 1) + b * BW
        fx = (pos % KW - KW // 2).astype(F32)
        fy = lax.div(pos, KW).astype(F32)
        rad = (fx * fx + fy * fy) / (KH * KH)
        tab = -jnp.sin(8.0 * defocus_ref[...] * rad + 0.1)
        zero = jnp.zeros((128 - 3 * CLASSES, BW), BF)
        hi, lo = split2(tab * tab)
        csq[b] = jnp.concatenate([hi, hi, lo, zero], axis=0)
        t1, t2, t3 = split3(tab)
        sel = dot(hot3_t, jnp.concatenate([t1, t2, t3, zero], axis=0))
        for bb in (b, b + HB):
            v = sel * img_ref[:, bb * BW:(bb + 1) * BW].astype(F32)
            hi, lo = split2(v)
            wh[bb] = hi
            wl[bb] = lo
    last = gather_a(m0, 0, first)
    last.wait_recv()
    pend.append(last)

    def place(b):
        q = lax.div(b, K)
        return lax.rem(q, 2), lax.rem(b, K), lax.div(q, 2)

    def rows_of(m, cc, k, uu):
        return jnp.concatenate([m[cc, k, uu, n // Z, n % Z] for n in range(X * Z)], axis=0)

    noise = noise_ref[...]

    for step in range(STEPS):
        sc_acc[...] = jnp.zeros_like(sc_acc)
        en_acc[...] = jnp.zeros_like(en_acc)

        def forward(b, carry):
            cc, k, uu = place(b)
            part = []
            for half in range(2):
                rows = rows_of(m0, cc, k, uu + half * (U // 2))
                v = dot(w3, jnp.concatenate(split3(rows), axis=0))
                plain[b + half * HB] = v
                part.append(v)
            re, im = part
            power = re * re + im * im
            hi, lo = split2(power)
            en_acc[...] += dot_t(hi, csq[b]) + dot_t(lo, csq[b])
            co, si_ = cosr[b], sinr[b]
            for half, v in enumerate((re * co - im * si_, re * si_ + im * co)):
                rh, rl = split2(v)
                bb = b + half * HB
                both = dot_t(jnp.concatenate([rh, rl], axis=0), wh[bb])
                sc_acc[...] += both[:NP] + both[NP:] + dot_t(rh, wl[bb])
            return carry

        lax.fori_loop(0, HB, forward, 0)
        e1, e2, e3 = split3(en_acc[...])
        picked = dot(e1, pick) + dot(e2, pick) + dot(e3, pick)
        scores = noise * (sc_acc[...] - 0.5 * picked)
        lpeak = jnp.max(scores, axis=0, keepdims=True)
        lsum = jnp.sum(jnp.exp(scores - lpeak), axis=0, keepdims=True)
        ebuf[step, p] = jnp.concatenate([lpeak, lsum, jnp.zeros((6, NI), F32)], axis=0)
        sent = [
            send(ebuf.at[step, p], ebuf.at[step, p], ev_s.at[step, n], ev_r.at[step, n], off)
            for n, off in enumerate(offs_e)
        ]
        for d in sent:
            d.wait()
        peak = lpeak
        for n in range(NPOSE):
            peak = jnp.maximum(peak, ebuf[step, n, 0:1, :])
        total = jnp.zeros_like(peak)
        for n in range(NPOSE):
            total += ebuf[step, n, 1:2, :] * jnp.exp(ebuf[step, n, 0:1, :] - peak)
        log_total = peak + jnp.log(total)
        usage = (noise * jnp.exp(scores - log_total)).astype(BF)
        use_ref[...] = usage
        mass = dot(usage, hot3_t)
        mh, ml = split2(mass)
        mcol = lax.broadcasted_iota(jnp.int32, mass.shape, 1)
        mass_ref[...] = jnp.where((mcol < CLASSES) | (mcol >= 2 * CLASSES), mh.astype(F32), ml.astype(F32)).astype(BF)

        def backward(cc, kc):
            def body(t, carry):
                k = kc * KB + lax.div(t, U // 2)
                uu = lax.rem(t, U // 2)
                b = (2 * uu + cc) * K + k
                use = use_ref[...]
                pr = dot(use, wh[b]) + dot(use, wl[b])
                pi = dot(use, wh[b + HB]) + dot(use, wl[b + HB])
                damp = dot(mass_ref[...], csq[b])
                co, si_ = cosr[b], sinr[b]
                outs = (
                    pr * co + pi * si_ - plain[b] * damp,
                    pi * co - pr * si_ - plain[b + HB] * damp,
                )
                for half, v in enumerate(outs):
                    hi, lo = split2(v)
                    g = dot(w_t2, jnp.concatenate([hi, lo], axis=0))
                    for n in range(X * Z):
                        grad[step, cc, k, uu + half * (U // 2), n // Z, n % Z] = g[n * R:(n + 1) * R]
                return carry

            lax.fori_loop(0, KB * (U // 2), body, 0)

        per = 1 + nb + nc
        oc = lax.rem(c + 1, 2)
        stage = []
        for kc in range(KC):
            backward(oc, kc)
            ks = pl.ds(kc * KB, KB)
            stage.append(send(grad.at[step, oc, ks], ra.at[step, ks],
                              rs_s.at[step, kc * per], rs_r.at[step, kc * per], offs_a[0]))
        slot = u * X + x
        stage_b = []
        for kc in range(KC):
            backward(c, kc)
            stage[kc].wait_recv()
            ks = pl.ds(kc * KB, KB)
            for k in range(kc * KB, (kc + 1) * KB):
                s1[step, k] = grad[step, c, k] + ra[step, k]
            ds = []
            for n, off in enumerate(offs_b):
                _, xx, uu, _ = coords(off)
                ds.append(send(s1.at[step, ks, uu, xx], rb.at[step, slot, ks],
                               rs_s.at[step, kc * per + 1 + n], rs_r.at[step, kc * per + 1 + n], off))
            rb[step, slot, ks] = s1[step, ks, u, x]
            stage_b.append(ds)
        stage_c = []
        for kc in range(KC):
            for d in stage_b[kc]:
                d.wait_recv()
            ks = pl.ds(kc * KB, KB)
            tot = rb[step, 0, ks]
            for n in range(1, U * X):
                tot += rb[step, n, ks]
            s2[step, ks] = tot
            ds = []
            for n, off in enumerate(offs_c):
                zz = coords(off)[0]
                ds.append(send(s2.at[step, ks, zz], rc.at[step, z, ks],
                               rs_s.at[step, kc * per + 1 + nb + n], rs_r.at[step, kc * per + 1 + nb + n], off))
            rc[step, z, ks] = s2[step, ks, z]
            stage_c.append(ds)
        for kc in range(KC):
            for d in stage_c[kc]:
                d.wait_recv()
            ks = pl.ds(kc * KB, KB)
            tot = rc[step, 0, ks]
            for n in range(1, Z):
                tot += rc[step, n, ks]
            own[ks] = tot
        pend.extend(stage)
        for ds in stage_b + stage_c:
            pend.extend(ds)

        if step < STEPS - 1:
            m1[c, :, u, x, z] = own[...]
            first = gather_start(m1, 1)
            first = gather_b(m1, 1, first)
            last = gather_a(m1, 1, first)
            last.wait_recv()
            pend.append(last)
            sq = jnp.zeros((R, BW), F32)
            for cc in range(2):
                for k in range(K):
                    for uu in range(U):
                        for n in range(X * Z):
                            v = m1[cc, k, uu, n // Z, n % Z]
                            sq += v * v
            spread = jnp.sqrt(jnp.sum(sq, keepdims=True) / (NS * F) + 1e-06)
            for d in pend:
                d.wait_send()
            pend.clear()
            for cc in range(2):
                for k in range(K):
                    for uu in range(U):
                        for n in range(X * Z):
                            at = (cc, k, uu, n // Z, n % Z)
                            m0[at] = m0[at] + 0.05 * m1[at] / spread
        else:
            g = own[...]
            mine = jnp.sum(jnp.sum(g * g, axis=0), keepdims=True)
            ta[c] = mine + jnp.zeros((8, 128), F32)
            d = send(ta.at[c], ta.at[c], t_s.at[0], t_r.at[0], offs_a[0])
            d.wait()
            tb[slot] = ta[0] + ta[1]
            ds = [send(tb.at[slot], tb.at[slot], t_s.at[1 + n], t_r.at[1 + n], off) for n, off in enumerate(offs_b)]
            for d in ds:
                d.wait()
            tot = tb[0]
            for n in range(1, U * X):
                tot += tb[n]
            tc[z] = tot
            ds = [send(tc.at[z], tc.at[z], t_s.at[1 + nb + n], t_r.at[1 + nb + n], off) for n, off in enumerate(offs_c)]
            for d in ds:
                d.wait()
            tot = tc[0]
            for n in range(1, Z):
                tot += tc[n]
            spread = jnp.sqrt(tot[0:1, 0:1] / (NS * F) + 1e-06)
            for k in range(K):
                out_ref[:, k * BW:(k + 1) * BW] = m0[c, k, u, x, z] + 0.05 * own[k] / spread
            share = NI // NPOSE
            ev = jnp.zeros((1, share), F32)
            for n in range(NPOSE):
                ev = jnp.where(p == n, log_total[:, n * share:(n + 1) * share], ev)
            ev_ref[...] = ev
    for d in pend:
        d.wait_send()


def shards(dims, images, inv_noise, defocus_class, defocus, pose_dir, pose_shift, slabs):
    X, Z, U, R, K, KC = dims
    ni, np_ = images.shape[0], pose_dir.shape[0]
    C = slabs.shape[1]
    npose = 2 * U
    nb, nc = U * X - 1, Z - 1
    vm = pltpu.VMEM
    dma = pltpu.SemaphoreType.DMA
    whole = (2, K, U, X, Z, R, BW)
    per = 1 + nb + nc
    scratch = [
        vm((NB, ni, BW), BF), vm((NB, ni, BW), BF),
        vm((HB, np_, BW), F32), vm((HB, np_, BW), F32),
        vm((HB, 128, BW), BF),
        vm((NB, np_, BW), F32),
        vm(whole, F32), vm(whole, F32),
        vm((STEPS,) + whole, F32),
        vm((STEPS,) + whole[1:], F32), vm((STEPS,) + whole[1:], F32),
        vm((STEPS, U * X, K, Z, R, BW), F32),
        vm((STEPS, K, Z, R, BW), F32),
        vm((STEPS, Z, K, R, BW), F32),
        vm((K, R, BW), F32),
        vm((STEPS, npose, 8, ni), F32),
        vm((2, 8, 128), F32), vm((U * X, 8, 128), F32), vm((Z, 8, 128), F32),
        vm((np_, ni), F32), vm((np_, 128), F32),
        vm((np_, ni), BF), vm((np_, 128), BF),
        dma((2, per)), dma((2, per)),
        dma((STEPS, KC * per)), dma((STEPS, KC * per)),
        dma((STEPS, npose)), dma((STEPS, npose)),
        dma((per,)), dma((per,)),
    ]
    out, ev = pl.pallas_call(
        functools.partial(kernel, dims),
        out_shape=(
            jax.ShapeDtypeStruct(slabs.shape, F32),
            jax.ShapeDtypeStruct((1, ni // npose), F32),
        ),
        in_specs=[pl.BlockSpec(memory_space=vm)] * 7,
        out_specs=(pl.BlockSpec(memory_space=vm),) * 2,
        scratch_shapes=scratch,
        compiler_params=pltpu.CompilerParams(
            collective_id=0, has_side_effects=True, vmem_limit_bytes=56 * 1024 * 1024
        ),
        cost_estimate=pl.CostEstimate(flops=8 * ni * np_ * F, bytes_accessed=2 * ni * F, transcendentals=0),
    )(
        images, inv_noise[None, :], defocus_class[None, :], defocus[:, None],
        pose_dir[None, :], pose_shift, slabs,
    )
    return out, ev[0]


def solution(mesh):
    n_img, n_pose = mesh.shape["img"], mesh.shape["pose"]
    X, Z, U = 2, n_img // 2, n_pose // 2
    R = NS // n_img
    K = F // n_pose // BW
    KC = 2 if K % 2 == 0 else 1
    in_specs = (
        P("img", None),
        P("img"),
        P("img"),
        P(),
        P("pose"),
        P("pose", None),
        P("img", "pose"),
    )
    out_specs = (P("img", "pose"), P(("img", "pose")))
    body = functools.partial(shards, (X, Z, U, R, K, KC))
    return jax.shard_map(body, mesh=mesh, in_specs=in_specs, out_specs=out_specs, check_vma=False)
```

time: 406 us -> 89.9 us (0.22)
  waiting for transfers between devices: 288 us -> 0 us
  Pallas kernels: 0 us -> 83.7 us
  matrix products: 40 us -> 0 us
  blocking collectives: 33.3 us -> 0 us
  other arithmetic: 26.9 us -> 0 us
  between operations: 15.3 us -> 0.64 us
  local copies, waits for them, and re-layouts: 0.62 us -> 5.3 us
    psum x2 -> x0, waiting for transfers between devices: 256 us -> none  [shards(): whole = lax.psum(gradient, ('img', 'pose'))]
    pallas_call x0 -> x1, Pallas kernels: none -> 83.7 us  [shards(): pl.pallas_call(functools.partial(kernel, dims), out_shape=(jax.ShapeDtype...]
    dot_general x17 -> x0, matrix products: 40 us -> none  [the longest x2 8.52 us: tile_scores(): lax.dot_general(weighted, references, (((1,), (1,)), ((), ())), precision...]
    all_gather x1 -> x0, waiting for transfers between devices: 31.9 us -> none  [assemble(): return lax.all_gather(columns, 'img', axis=0, tiled=True)]
    sub x5 -> x0, other arithmetic: 17.3 us -> none  [the longest x4 16.6 us: rotate(): real_part * cosine - imag_part * sine]
    psum x2 -> x0, blocking collectives: 13.6 us -> none  [pose_evidence(): total = lax.psum(jnp.sum(jnp.exp(scores - peak[:, None]), axis=1), 'pose')]
    pmax x2 -> x0, blocking collectives: 11.3 us -> none  [pose_evidence(): peak = lax.pmax(jnp.max(scores, axis=1), 'pose')]
    all_gather x1 -> x0, blocking collectives: 8.37 us -> none  [assemble(): columns = lax.all_gather(own_map, 'pose', axis=1, tiled=True)]
  transfers between devices with their start and end apart: 3 -> 0, of which waited for: 3 -> 0; matrix products, arithmetic and copies ran while one was open for 2% -> 0% of each run, Pallas kernels for 0% -> 0%
where the time goes in v1:
time: 89.9 us; the launch traced here: 89.6 us
  Pallas kernels  83.7 us (93%)
  local copies, waits for them, and re-layouts  5.3 us (6%)
    pallas_call x1, Pallas kernels, shards(): pl.pallas_call(functools.partial(kernel, dims), out_shape=(jax.ShapeDtype...  83.7 us
    unnamed x3, local copies, waits for them, and re-layouts  3.97 us

profile of v1, /device:TPU:0, one launch (start us, length us, event | category | flops | bytes accessed | tf_op | source)
XLA Modules:
  0.0 89.6 jit_solution(1309691423323506281)
XLA Ops:
  0.6 1.3 %copy.9.defocus_ref = f32[16,1]{1,0:T(8,128)} copy(f32[16,1]{0,1:T(1,128)} %bitcast.5) | data formatting | bytes 128 | tf_op jit(solution)/shard_map/broadcast_in_dim | solution.py:409
  2.0 1.4 %copy.10.shift_ref = s32[128,2]{1,0:T(8,128)} copy(s32[128,2]{0,1:T(2,128)} %param.12) | data formatting | bytes 2048 | tf_op args[5]
  3.4 83.7 %shard_map.86 = (f32[8,1024]{1,0:T(8,128)}, f32[1,64]{1,0:T(1,128)}) custom-call(bf16[256,4096]{1,0:T(8,128)(2,1)} %img_ref.1, f32[1,256]{1,0:T(1,128)} %bitcast.6, s32[1,256]{1,0:T(1,128)} %bitcast.7, f32[16,1]{1,0:T(8,128)} %copy.9.defocus_ref, s32[1,128]{1,0:T(1,128)} %bitcast.8, s32[128,2]{1,0:T(8,128)} %copy.10.shift_ref, f32[8,1024]{1,0:T(8,128)} %slab_ref.1), custom_call_target="tpu_custom_call" | custom-call | flops 1073741824 | bytes 2097152 | tf_op jit(solution)/shard_map/pallas_call | solution.py:395
  87.0 1.4 %copy.13 = f32[8,1024]{1,0:T(8,128)} copy(f32[8,1024]{1,0:T(8,128)} %get-tuple-element.8) | data formatting | bytes 65536
  88.4 1.2 %copy.14 = f32[64]{0:T(128)} copy(f32[64]{0:T(128)} %bitcast.9) | data formatting | bytes 512

commit v2 on v1

--- a/solution.py
+++ b/solution.py
@@ -49,10 +49,10 @@
     img_ref, noise_ref, class_ref, defocus_ref, dir_ref, shift_ref, slab_ref,
     out_ref, ev_ref,
     wh, wl, cosr, sinr, csq, plain, m0, m1, grad, ra, s1, rb, s2, rc, own,
-    ebuf, ta, tb, tc, sc_acc, en_acc, use_ref, mass_ref,
+    ebuf, ta, tb, sc_acc, en_acc, use_ref, mass_ref,
     ag_s, ag_r, rs_s, rs_r, ev_s, ev_r, t_s, t_r,
 ):
-    (X, Z, U, R, K, KC) = dims
+    (X, Z, U, R, K, KC, KG) = dims
     KB = K // KC
     NI = img_ref.shape[0]
     NP = dir_ref.shape[1]
@@ -73,8 +73,10 @@
     offs_b = [(0, dx, du, 0) for du in range(U) for dx in range(X) if du or dx]
     offs_c = [(dz, 0, 0, 0) for dz in range(1, Z)]
     offs_e = [(0, 0, du, dc) for du in range(U) for dc in range(2) if du or dc]
-    everyone = sorted(set(offs_a + offs_b + offs_c + offs_e))
+    offs_i = [(dz, dx, 0, 0) for dz in range(Z) for dx in range(X) if dz or dx]
+    everyone = sorted(set(offs_a + offs_b + offs_c + offs_e + offs_i))
     nb, nc = len(offs_b), len(offs_c)
+    per = 1 + nb + nc
 
     barrier = pltpu.get_barrier_semaphore()
     for off in everyone:
@@ -91,26 +93,43 @@
 
     pend = []
 
+    def part(k):
+        return pl.ds(k * (K // KG), K // KG)
+
     def gather_start(m, g):
         return [
-            send(m.at[c, :, u, x, z], m.at[c, :, u, x, z], ag_s.at[g, n], ag_r.at[g, n], off)
-            for n, off in enumerate(offs_c)
+            [
+                send(m.at[c, part(k), u, x, z], m.at[c, part(k), u, x, z],
+                     ag_s.at[g, k * per + n], ag_r.at[g, k * per + n], off)
+                for n, off in enumerate(offs_c)
+            ]
+            for k in range(KG)
         ]
 
     def gather_b(m, g, first):
-        for d in first:
+        out = []
+        for k in range(KG):
+            for d in first[k]:
+                d.wait_recv()
+            pend.extend(first[k])
+            out.append([
+                send(m.at[c, part(k), u, x], m.at[c, part(k), u, x],
+                     ag_s.at[g, k * per + nc + n], ag_r.at[g, k * per + nc + n], off)
+                for n, off in enumerate(offs_b)
+            ])
+        return out
+
+    def gather_a(m, g, second):
+        out = []
+        for k in range(KG):
+            for d in second[k]:
+                d.wait_recv()
+            pend.extend(second[k])
+            at = k * per + nc + nb
+            out.append(send(m.at[c, part(k)], m.at[c, part(k)], ag_s.at[g, at], ag_r.at[g, at], offs_a[0]))
+        for d in out:
             d.wait_recv()
-        pend.extend(first)
-        return [
-            send(m.at[c, :, u, x], m.at[c, :, u, x], ag_s.at[g, nc + n], ag_r.at[g, nc + n], off)
-            for n, off in enumerate(offs_b)
-        ]
-
-    def gather_a(m, g, second):
-        for d in second:
-            d.wait_recv()
-        pend.extend(second)
-        return send(m.at[c], m.at[c], ag_s.at[g, nc + nb], ag_r.at[g, nc + nb], offs_a[0])
+        pend.extend(out)
 
     for k in range(K):
         m0[c, k, u, x, z] = slab_ref[:, k * BW:(k + 1) * BW]
@@ -139,8 +158,10 @@
     first = gather_b(m0, 0, first)
 
     lane = lax.broadcasted_iota(jnp.int32, (NP, 128), 1)
-    shx = shift_ref[:, 0:1]
-    shy = shift_ref[:, 1:2]
+    shx, shy = [
+        (shift_ref[n:n + 1, :].astype(F32) + jnp.zeros((128, NP), F32)).T.astype(jnp.int32)
+        for n in range(2)
+    ]
     turn = 2.0 * math.pi / (4 * KH)
     base = turn * (shx * (lane % KW - KW // 2) + shy * lax.div(lane, KW)).astype(F32)
     inc = turn * (2 * shy + 0 * lane).astype(F32)
@@ -151,12 +172,15 @@
         sinr[b, :, h:h + 128] = sb
         cb, sb = cb * ci - sb * si, sb * ci + cb * si
 
+    same = lax.broadcasted_iota(jnp.int32, (CLASSES, CLASSES), 0) == lax.broadcasted_iota(
+        jnp.int32, (CLASSES, CLASSES), 1)
+    blur = jnp.sum(jnp.where(same, defocus_ref[...], 0.0), axis=1, keepdims=True)
     for b in range(HB):
         pos = lax.broadcasted_iota(jnp.int32, (CLASSES, BW), 1) + b * BW
         fx = (pos % KW - KW // 2).astype(F32)
         fy = lax.div(pos, KW).astype(F32)
         rad = (fx * fx + fy * fy) / (KH * KH)
-        tab = -jnp.sin(8.0 * defocus_ref[...] * rad + 0.1)
+        tab = -jnp.sin(8.0 * blur * rad + 0.1)
         zero = jnp.zeros((128 - 3 * CLASSES, BW), BF)
         hi, lo = split2(tab * tab)
         csq[b] = jnp.concatenate([hi, hi, lo, zero], axis=0)
@@ -167,9 +191,7 @@
             hi, lo = split2(v)
             wh[bb] = hi
             wl[bb] = lo
-    last = gather_a(m0, 0, first)
-    last.wait_recv()
-    pend.append(last)
+    gather_a(m0, 0, first)
 
     def place(b):
         q = lax.div(b, K)
@@ -254,7 +276,6 @@
 
             lax.fori_loop(0, KB * (U // 2), body, 0)
 
-        per = 1 + nb + nc
         oc = lax.rem(c + 1, 2)
         stage = []
         for kc in range(KC):
@@ -309,9 +330,7 @@
             m1[c, :, u, x, z] = own[...]
             first = gather_start(m1, 1)
             first = gather_b(m1, 1, first)
-            last = gather_a(m1, 1, first)
-            last.wait_recv()
-            pend.append(last)
+            gather_a(m1, 1, first)
             sq = jnp.zeros((R, BW), F32)
             for cc in range(2):
                 for k in range(K):
@@ -332,23 +351,20 @@
         else:
             g = own[...]
             mine = jnp.sum(jnp.sum(g * g, axis=0), keepdims=True)
-            ta[c] = mine + jnp.zeros((8, 128), F32)
-            d = send(ta.at[c], ta.at[c], t_s.at[0], t_r.at[0], offs_a[0])
-            d.wait()
-            tb[slot] = ta[0] + ta[1]
-            ds = [send(tb.at[slot], tb.at[slot], t_s.at[1 + n], t_r.at[1 + n], off) for n, off in enumerate(offs_b)]
+            ta[p] = mine + jnp.zeros((8, 128), F32)
+            ds = [send(ta.at[p], ta.at[p], t_s.at[n], t_r.at[n], off) for n, off in enumerate(offs_e)]
+            for d in ds:
+                d.wait()
+            tot = ta[0]
+            for n in range(1, NPOSE):
+                tot += ta[n]
+            tb[i] = tot
+            ds = [send(tb.at[i], tb.at[i], t_s.at[NPOSE + n], t_r.at[NPOSE + n], off) for n, off in enumerate(offs_i)]
             for d in ds:
                 d.wait()
             tot = tb[0]
-            for n in range(1, U * X):
+            for n in range(1, X * Z):
                 tot += tb[n]
-            tc[z] = tot
-            ds = [send(tc.at[z], tc.at[z], t_s.at[1 + nb + n], t_r.at[1 + nb + n], off) for n, off in enumerate(offs_c)]
-            for d in ds:
-                d.wait()
-            tot = tc[0]
-            for n in range(1, Z):
-                tot += tc[n]
             spread = jnp.sqrt(tot[0:1, 0:1] / (NS * F) + 1e-06)
             for k in range(K):
                 out_ref[:, k * BW:(k + 1) * BW] = m0[c, k, u, x, z] + 0.05 * own[k] / spread
@@ -362,7 +378,7 @@
 
 
 def shards(dims, images, inv_noise, defocus_class, defocus, pose_dir, pose_shift, slabs):
-    X, Z, U, R, K, KC = dims
+    X, Z, U, R, K, KC, KG = dims
     ni, np_ = images.shape[0], pose_dir.shape[0]
     C = slabs.shape[1]
     npose = 2 * U
@@ -384,13 +400,13 @@
         vm((STEPS, Z, K, R, BW), F32),
         vm((K, R, BW), F32),
         vm((STEPS, npose, 8, ni), F32),
-        vm((2, 8, 128), F32), vm((U * X, 8, 128), F32), vm((Z, 8, 128), F32),
+        vm((npose, 8, 128), F32), vm((X * Z, 8, 128), F32),
         vm((np_, ni), F32), vm((np_, 128), F32),
         vm((np_, ni), BF), vm((np_, 128), BF),
-        dma((2, per)), dma((2, per)),
+        dma((2, KG * per)), dma((2, KG * per)),
         dma((STEPS, KC * per)), dma((STEPS, KC * per)),
         dma((STEPS, npose)), dma((STEPS, npose)),
-        dma((per,)), dma((per,)),
+        dma((npose + X * Z,)), dma((npose + X * Z,)),
     ]
     out, ev = pl.pallas_call(
         functools.partial(kernel, dims),
@@ -406,8 +422,8 @@
         ),
         cost_estimate=pl.CostEstimate(flops=8 * ni * np_ * F, bytes_accessed=2 * ni * F, transcendentals=0),
     )(
-        images, inv_noise[None, :], defocus_class[None, :], defocus[:, None],
-        pose_dir[None, :], pose_shift, slabs,
+        images, inv_noise[None, :], defocus_class[None, :], defocus[None, :],
+        pose_dir[None, :], pose_shift.T, slabs,
     )
     return out, ev[0]
 
@@ -417,7 +433,8 @@
     X, Z, U = 2, n_img // 2, n_pose // 2
     R = NS // n_img
     K = F // n_pose // BW
-    KC = 2 if K % 2 == 0 else 1
+    KC = K
+    KG = 2 if K % 2 == 0 else 1
     in_specs = (
         P("img", None),
         P("img"),
@@ -428,5 +445,5 @@
         P("img", "pose"),
     )
     out_specs = (P("img", "pose"), P(("img", "pose")))
-    body = functools.partial(shards, (X, Z, U, R, K, KC))
+    body = functools.partial(shards, (X, Z, U, R, K, KC, KG))
     return jax.shard_map(body, mesh=mesh, in_specs=in_specs, out_specs=out_specs, check_vma=False)

time: 89.9 us -> 83.5 us (0.929)
  Pallas kernels: 83.7 us -> 80 us
  local copies, waits for them, and re-layouts: 5.3 us -> 2.55 us
    pallas_call x1, Pallas kernels: 83.7 us -> 80 us  [shards(): pl.pallas_call(functools.partial(kernel, dims), out_shape=(jax.ShapeDtype...]
    unnamed x3 -> x2, local copies, waits for them, and re-layouts: 3.97 us -> 2.55 us
    broadcast_in_dim x1 -> x0, local copies, waits for them, and re-layouts: 1.33 us -> none  [shards(): defocus[:, None]]
where the time goes in v2:
time: 83.5 us; the launch traced here: 83.2 us
  Pallas kernels  80 us (96%)
  local copies, waits for them, and re-layouts  2.55 us (3%)
    pallas_call x1, Pallas kernels, shards(): pl.pallas_call(functools.partial(kernel, dims), out_shape=(jax.ShapeDtype...  80 us
    unnamed x2, local copies, waits for them, and re-layouts  2.55 us

profile of v2, /device:TPU:0, one launch (start us, length us, event | category | flops | bytes accessed | tf_op | source)
XLA Modules:
  0.0 83.2 jit_solution(16958310530750549335)
XLA Ops:
  0.6 80.0 %shard_map.86 = (f32[8,1024]{1,0:T(8,128)}, f32[1,64]{1,0:T(1,128)}) custom-call(bf16[256,4096]{1,0:T(8,128)(2,1)} %img_ref.1, f32[1,256]{1,0:T(1,128)} %bitcast.6, s32[1,256]{1,0:T(1,128)} %bitcast.7, f32[1,16]{1,0:T(1,128)} %bitcast.9, s32[1,128]{1,0:T(1,128)} %bitcast.10, s32[2,128]{1,0:T(2,128)} %bitcast.8, f32[8,1024]{1,0:T(8,128)} %slab_ref.1), custom_call_target="tpu_custom_call" | custom-call | flops 1073741824 | bytes 2097152 | tf_op jit(solution)/shard_map/pallas_call | solution.py:411
  80.7 1.4 %copy.11 = f32[8,1024]{1,0:T(8,128)} copy(f32[8,1024]{1,0:T(8,128)} %get-tuple-element.8) | data formatting | bytes 65536
  82.0 1.2 %copy.12 = f32[64]{0:T(128)} copy(f32[64]{0:T(128)} %bitcast.11) | data formatting | bytes 512
